TPU v7x, 256 devices: a whole 4x4x8 slice. The times are simulated.
256 devices in a mesh: dp: 32 (over y, z), hg: 8 (over x, core).
Axes of the slice: x: 4, y: 4, z: 8, core: 2. Of those that a mesh axis runs over, the one named last changes fastest.
Arguments:
- w_ukv: bfloat16 [512, 32768], P('dp', 'hg'), may hold values from -1 to 1
- w_uq: bfloat16 [1536, 16384], P('dp', 'hg'), may hold values from -1 to 1
- query_latent: bfloat16 [2, 1024, 1536], P(None, 'dp'), may hold values from -6 to 6
- new_latent: bfloat16 [2, 1024, 512], P(None, 'dp'), may hold values from -12 to 12
- latent_cache: bfloat16 [2048, 128, 512], P('dp'), may hold values from -12 to 12
- cache_lengths: int32 [2048], P('dp'), may hold values from 16 to 128, as said below
- owners: int32 [1024, 1], P('dp'), may hold values from 0 to 31; in each aligned block of 32 rows (0 to 31, 32 to 63, ...) at most 2 rows name the same one
Outputs:
- attention_out: bfloat16 [2, 1024, 16384], P(None, 'dp', 'hg')
Inputs may be any that keep to these rules, and one draw needn't show every extreme that they name: `owners`: among the 32 requests of one dp rank no owner is named more than 2 times, a bound that some block reaches. `cache_lengths`: some slot holds exactly 128 tokens.
All inputs are finite; a program needn't handle non-finite values.
Results may differ from a plain program's by a relative error of at most 0.008.
Values may be sent and summed in bfloat16 or wider, within the bound.
A program may use at most 128 MiB of HBM per device.

v0:
```python
import jax
import jax.numpy as jnp
from jax import lax
from jax.sharding import PartitionSpec as P

C = 512
NOPE = 128
VDIM = 128
QRANK = 1536
STEPS = 2


def head_absorb(row_block, key_heads, head_count):
    blocks = row_block.reshape(row_block.shape[0], head_count, NOPE).transpose(1, 0, 2)

    def one_head(operands):
        return jnp.dot(operands[0], operands[1].T, preferred_element_type=jnp.float32).astype(
            jnp.bfloat16
        )

    return lax.map(one_head, (blocks, key_heads))


def local(w_ukv, w_uq, query_latent, new_latent, latent_cache, cache_lengths, owners):
    dp_count = lax.axis_size("dp")
    head_count = w_uq.shape[1] // NOPE
    slot_count = latent_cache.shape[0]
    send_cap = slot_count // dp_count
    gathered = lax.all_gather(w_ukv, "dp", axis=0, tiled=True).reshape(C, head_count, NOPE + VDIM)
    key_heads = gathered[:, :, :NOPE].transpose(1, 0, 2)
    value_up = gathered[:, :, NOPE:]
    absorbed = head_absorb(lax.all_gather(w_uq, "dp", axis=0, tiled=True), key_heads, head_count)
    owner_rank = owners[:, 0]
    onehot = (owner_rank[:, None] == jnp.arange(dp_count, dtype=jnp.int32)[None, :]).astype(
        jnp.int32
    )
    before = jnp.cumsum(onehot, 0) - onehot
    destination = owner_rank * send_cap + jnp.sum(before * onehot, 1)
    placement_map = (
        jnp.arange(slot_count, dtype=jnp.int32)[:, None] == destination[None, :]
    ).astype(jnp.bfloat16)
    valid_mask = (
        jnp.arange(latent_cache.shape[1], dtype=jnp.int32)[None, :] < cache_lengths[:, None]
    )
    score_scale = NOPE ** (-0.5)
    fresh_list = []
    results = []
    for step_index in range(STEPS):
        payload = jnp.concatenate([query_latent[step_index], new_latent[step_index]], 1)
        outgoing = jnp.dot(placement_map, payload, preferred_element_type=jnp.float32).astype(
            jnp.bfloat16
        )
        outgoing = outgoing.reshape(dp_count, send_cap, QRANK + C)
        arrived = lax.all_to_all(outgoing, "dp", split_axis=0, concat_axis=0, tiled=True)
        arrived = arrived.reshape(slot_count, QRANK + C)
        queries = arrived[:, :QRANK]
        fresh_list.append(arrived[:, QRANK:])
        fresh_stack = jnp.stack(fresh_list, 1)
        query_abs = jnp.einsum(
            "sq,hqc->shc", queries, absorbed, preferred_element_type=jnp.float32
        ).astype(jnp.bfloat16)
        cache_scores = (
            jnp.einsum("shc,stc->sht", query_abs, latent_cache, preferred_element_type=jnp.float32)
            * score_scale
        )
        cache_scores = jnp.where(valid_mask[:, None, :], cache_scores, -1e30)
        fresh_scores = (
            jnp.einsum("shc,sjc->shj", query_abs, fresh_stack, preferred_element_type=jnp.float32)
            * score_scale
        )
        peak_score = jnp.maximum(jnp.max(cache_scores, 2), jnp.max(fresh_scores, 2))
        cache_exp = jnp.exp(cache_scores - peak_score[:, :, None])
        fresh_exp = jnp.exp(fresh_scores - peak_score[:, :, None])
        denominator = jnp.sum(cache_exp, 2) + jnp.sum(fresh_exp, 2)
        cache_weight = (cache_exp / denominator[:, :, None]).astype(jnp.bfloat16)
        fresh_weight = (fresh_exp / denominator[:, :, None]).astype(jnp.bfloat16)
        mixed_latent = jnp.einsum(
            "sht,stc->shc", cache_weight, latent_cache, preferred_element_type=jnp.float32
        )
        mixed_latent = mixed_latent + jnp.einsum(
            "shj,sjc->shc", fresh_weight, fresh_stack, preferred_element_type=jnp.float32
        )
        mixed_latent = mixed_latent.astype(jnp.bfloat16)
        head_out = jnp.einsum(
            "shc,chv->shv", mixed_latent, value_up, preferred_element_type=jnp.float32
        ).astype(jnp.bfloat16)
        head_out = head_out.reshape(dp_count, send_cap, head_count * VDIM)
        returned = lax.all_to_all(head_out, "dp", split_axis=0, concat_axis=0, tiled=True).reshape(
            slot_count, head_count * VDIM
        )
        own_rows = jnp.dot(placement_map.T, returned, preferred_element_type=jnp.float32).astype(
            jnp.bfloat16
        )
        results.append(own_rows)
    return jnp.stack(results, 0)


def solution(mesh):
    in_specs = (
        P("dp", "hg"),
        P("dp", "hg"),
        P(None, "dp", None),
        P(None, "dp", None),
        P("dp", None, None),
        P("dp"),
        P("dp", None),
    )
    out_specs = P(None, "dp", "hg")
    return jax.shard_map(local, mesh=mesh, in_specs=in_specs, out_specs=out_specs, check_vma=False)
```

profile of v0, /device:TPU:2, one launch (start us, length us, event | category | flops | bytes accessed | tf_op | source)
XLA Modules:
  0.0 314.1 jit_solution(1636127709758357835)
XLA Ops:
  6.5 0.7 all-gather.5.cloned.1.call-update
  7.3 0.7 all-gather.3.cloned.1.call-update
  8.0 0.7 fusion.58
  8.8 0.8 select_reduce_fusion
  9.6 0.7 multiply_add_fusion
  10.3 0.8 slice_bitcast_fusion.11
  11.1 1.0 slice_bitcast_fusion.6
  12.0 0.2 convolution_convert_fusion.1
  12.2 0.9 reshape.93
  13.1 11.5 %all-to-all-start.2 = ((bf16[32,2,2048]{2,1,0:T(2,128)(2,1)}), bf16[32,2,2048]{2,1,0:T(2,128)(2,1)S(1)}, u32[]{:S(2)}, u32[]{:S(2)}) async-start(bf16[32,2,2048]{2,1,0:T(2,128)(2,1)} %reshape.93), calls=%async_computation.2 | async-start | bytes 524288 | tf_op jit(solution)/shard_map/all_to_all | solution.py:54
  24.6 0.2 convolution_convert_fusion.2
  24.8 0.9 reshape.87
  25.7 12.2 %all-to-all-done.2 = bf16[32,2,2048]{2,1,0:T(2,128)(2,1)S(1)} async-done(((bf16[32,2,2048]{2,1,0:T(2,128)(2,1)}), bf16[32,2,2048]{2,1,0:T(2,128)(2,1)S(1)}, u32[]{:S(2)}, u32[]{:S(2)}) %all-to-all-start.2) | async-done | bytes 262176 | tf_op jit(solution)/shard_map/all_to_all | solution.py:54
  38.0 4.9 %all-to-all-start = ((bf16[32,2,2048]{2,1,0:T(2,128)(2,1)}), bf16[32,2,2048]{2,1,0:T(2,128)(2,1)S(1)}, u32[]{:S(2)}, u32[]{:S(2)}) async-start(bf16[32,2,2048]{2,1,0:T(2,128)(2,1)} %reshape.87), calls=%async_computation | async-start | bytes 524288 | tf_op jit(solution)/shard_map/all_to_all | solution.py:54
  42.8 0.7 iota_compare_fusion
  43.6 0.1 reshape.94
  43.7 11.4 %all-to-all-done = bf16[32,2,2048]{2,1,0:T(2,128)(2,1)S(1)} async-done(((bf16[32,2,2048]{2,1,0:T(2,128)(2,1)}), bf16[32,2,2048]{2,1,0:T(2,128)(2,1)S(1)}, u32[]{:S(2)}, u32[]{:S(2)}) %all-to-all-start) | async-done | bytes 262176 | tf_op jit(solution)/shard_map/all_to_all | solution.py:54
  55.3 40.3 %all-gather.5.cloned.1.call-done = bf16[512,4096]{1,0:T(8,128)(2,1)} async-done(((bf16[16,4096]{1,0:T(8,128)(2,1)}), bf16[512,4096]{1,0:T(8,128)(2,1)}) %all-gather.5.cloned.1.call-update) | async-done | bytes 4194320 | tf_op jit(solution)/shard_map/all_gather | solution.py:29
  95.6 6.5 %copy.26 = bf16[512,4096]{0,1:T(8,128)(2,1)} copy(bf16[512,4096]{1,0:T(8,128)(2,1)} %all-gather.5.cloned.1.call-done) | data formatting | bytes 8388608 | tf_op jit(solution)/shard_map/all_gather | solution.py:29
  102.0 1.8 slice_bitcast_fusion
  103.8 80.3 %all-gather.3.cloned.1.call-done = bf16[1536,2048]{1,0:T(8,128)(2,1)} async-done(((bf16[48,2048]{1,0:T(8,128)(2,1)}), bf16[1536,2048]{1,0:T(8,128)(2,1)}) %all-gather.3.cloned.1.call-update) | async-done | bytes 6291472 | tf_op jit(solution)/shard_map/all_gather | solution.py:32
  184.2 8.6 %copy.25 = bf16[1536,2048]{0,1:T(8,128)(2,1)} copy(bf16[1536,2048]{1,0:T(8,128)(2,1)} %all-gather.3.cloned.1.call-done) | data formatting | bytes 12582912 | tf_op jit(solution)/shard_map/all_gather | solution.py:32
  192.8 44.0 %while.10 = (s32[]{:T(128)}, bf16[16,1536,512]{2,1,0:T(8,128)(2,1)}, bf16[16,1536,128]{1,2,0:T(8,128)(2,1)}, bf16[16,512,128]{1,2,0:T(8,128)(2,1)S(1)}, s32[]{:T(128)}) while((s32[]{:T(128)}, bf16[16,1536,512]{2,1,0:T(8,128)(2,1)}, bf16[16,1536,128]{1,2,0:T(8,128)(2,1)}, bf16[16,512,128]{1,2,0:T(8,128)(2,1)S(1)}, s32[]{:T(128)}) %tuple.35), condition=%wide.region_3.4_spmd, body=%wide.region_2.3_spmd.sunk | while | flops 202113024 | bytes 2098757 | solution.py:21
  192.8 2.8 fusion.78
  195.5 2.7 fusion.78
  198.3 2.7 fusion.78
  201.0 2.8 fusion.78
  203.8 2.7 fusion.78
  206.5 2.8 fusion.78
  209.3 2.8 fusion.78
  212.0 2.7 fusion.78
  214.8 2.8 fusion.78
  217.6 2.7 fusion.78
  220.3 2.7 fusion.78
  223.0 2.8 fusion.78
  225.8 2.7 fusion.78
  228.5 2.7 fusion.78
  231.2 2.8 fusion.78
  234.0 2.7 fusion.78
  236.8 10.7 %convolution_convert_fusion.5 = bf16[64,16,512]{2,0,1:T(8,128)(2,1)S(1)} fusion(bf16[16,1536,512]{2,1,0:T(8,128)(2,1)} %get-tuple-element.27, bf16[64,2048]{1,0:T(8,128)(2,1)S(1)} %reshape.94), kind=kOutput, calls=%fused_computation.21 | convolution fusion | flops 1611137024 | bytes 26411008 | tf_op jit(solution)/shard_map/sq,hqc->shc/dot_general | solution.py:59
  247.5 10.7 %convolution_convert_fusion.6 = bf16[64,16,512]{2,0,1:T(8,128)(2,1)S(1)} fusion(bf16[16,1536,512]{2,1,0:T(8,128)(2,1)} %get-tuple-element.27, bf16[64,2048]{1,0:T(8,128)(2,1)S(1)} %reshape.88), kind=kOutput, calls=%fused_computation.22 | convolution fusion | flops 1611137024 | bytes 26411008 | tf_op jit(solution)/shard_map/sq,hqc->shc/dot_general | solution.py:59
  258.3 0.8 fusion.63
  259.1 2.4 fusion.62
  261.5 0.4 fusion.35
  261.8 0.1 fusion.50
  262.0 1.3 fusion.36
  263.2 0.5 add_convert_fusion
  263.8 0.4 copy-done
  264.2 0.9 fusion.24
  265.0 0.2 copy.38
  265.2 0.8 reshape.95
  266.0 5.7 %all-to-all-start.3 = ((bf16[32,2,2048]{2,1,0:T(2,128)(2,1)}), bf16[32,2,2048]{2,1,0:T(2,128)(2,1)S(1)}, u32[]{:S(2)}, u32[]{:S(2)}) async-start(bf16[32,2,2048]{2,1,0:T(2,128)(2,1)} %reshape.95), calls=%async_computation.3 | async-start | bytes 524288 | tf_op jit(solution)/shard_map/all_to_all | solution.py:88
  271.7 5.7 %fusion.64 = (f32[64,16]{1,0:T(8,128)S(1)}, f32[64,16,128]{2,1,0:T(8,128)S(1)}) fusion(bf16[64,128,512]{2,1,0:T(8,128)(2,1)} %param.13, bf16[64,16,512]{2,0,1:T(8,128)(2,1)S(1)} %convolution_convert_fusion.6, pred[64,128]{1,0:T(8,128)(4,1)S(1)} %iota_compare_fusion), kind=kOutput, calls=%fused_computation.95 | convolution fusion | flops 134609920 | bytes 9973760 | tf_op jit(solution)/shard_map/shc,stc->sht/dot_general | solution.py:63
  277.4 0.7 fusion.31
  278.1 0.4 fusion.34
  278.6 4.8 %add_convert_fusion.1 = bf16[64,16,512]{2,1,0:T(8,128)(2,1)S(1)} fusion(bf16[64,128,512]{2,1,0:T(8,128)(2,1)} %param.13, f32[64,512]{1,0:T(8,128)S(1)} %get-tuple-element.45, f32[64,16]{1,0:T(8,128)S(1)} %get-tuple-element.50, f32[64,16,128]{2,1,0:T(8,128)S(1)} %get-tuple-element.58, f32[64,16]{1,0:T(8,128)S(1)} %get-tuple-element.49, ...), kind=kOutput, calls=%fused_computation.16 | convolution fusion | flops 136183808 | bytes 10104832 | tf_op jit(solution)/shard_map/sht,stc->shc/dot_general | solution.py:77
  283.4 0.8 fusion.21
  284.2 0.2 copy.32
  284.4 0.8 reshape.91
  285.1 9.6 %all-to-all-start.1 = ((bf16[32,2,2048]{2,1,0:T(2,128)(2,1)}), bf16[32,2,2048]{2,1,0:T(2,128)(2,1)S(1)}, u32[]{:S(2)}, u32[]{:S(2)}) async-start(bf16[32,2,2048]{2,1,0:T(2,128)(2,1)} %reshape.91), calls=%async_computation.1 | async-start | bytes 524288 | tf_op jit(solution)/shard_map/all_to_all | solution.py:88
  294.9 0.2 fusion.8
  295.1 11.1 %all-to-all-done.1 = bf16[32,2,2048]{2,1,0:T(2,128)(2,1)S(1)} async-done(((bf16[32,2,2048]{2,1,0:T(2,128)(2,1)}), bf16[32,2,2048]{2,1,0:T(2,128)(2,1)S(1)}, u32[]{:S(2)}, u32[]{:S(2)}) %all-to-all-start.1) | async-done | bytes 262176 | tf_op jit(solution)/shard_map/all_to_all | solution.py:88
  306.3 0.2 fusion.7
  306.6 0.7 pad_maximum_fusion
  (23 shorter events, 0.5 us)
Async XLA Ops:
  6.5 89.0 %all-gather.5.cloned.1.call-start = ((), (), s32[]{:S(2)}) async-start(), calls=%async_computation.5 | async-start | bytes 4325376 | tf_op jit(solution)/shard_map/all_gather | solution.py:29
  7.3 176.9 %all-gather.3.cloned.1.call-start = ((), (), s32[]{:S(2)}) async-start(), calls=%async_computation.4 | async-start | bytes 6488064 | tf_op jit(solution)/shard_map/all_gather | solution.py:32
  13.1 24.8 %all-to-all-start.2 = ((bf16[32,2,2048]{2,1,0:T(2,128)(2,1)}), bf16[32,2,2048]{2,1,0:T(2,128)(2,1)S(1)}, u32[]{:S(2)}, u32[]{:S(2)}) async-start(bf16[32,2,2048]{2,1,0:T(2,128)(2,1)} %reshape.93), calls=%async_computation.2 | async-start | bytes 524288 | tf_op jit(solution)/shard_map/all_to_all | solution.py:54
  38.0 17.1 %all-to-all-start = ((bf16[32,2,2048]{2,1,0:T(2,128)(2,1)}), bf16[32,2,2048]{2,1,0:T(2,128)(2,1)S(1)}, u32[]{:S(2)}, u32[]{:S(2)}) async-start(bf16[32,2,2048]{2,1,0:T(2,128)(2,1)} %reshape.87), calls=%async_computation | async-start | bytes 524288 | tf_op jit(solution)/shard_map/all_to_all | solution.py:54
  236.8 22.3 %slice-start = ((s8[8388608]{0:T(1024)(128)(4,1)}), s8[4194304]{0:T(1024)(128)(4,1)S(1)}, s32[]{:S(2)}) async-start(s8[8388608]{0:T(1024)(128)(4,1)} %bitcast.64), calls=%async_computation.6 | async-start | bytes 8388608
  247.5 11.6 %slice-start.1 = ((s8[8388608]{0:T(1024)(128)(4,1)}), s8[4194304]{0:T(1024)(128)(4,1)S(1)}, s32[]{:S(2)}) async-start(s8[8388608]{0:T(1024)(128)(4,1)} %bitcast.64), calls=%async_computation.7 | async-start | bytes 8388608
  262.0 2.2 copy-start
  266.0 19.2 %all-to-all-start.3 = ((bf16[32,2,2048]{2,1,0:T(2,128)(2,1)}), bf16[32,2,2048]{2,1,0:T(2,128)(2,1)S(1)}, u32[]{:S(2)}, u32[]{:S(2)}) async-start(bf16[32,2,2048]{2,1,0:T(2,128)(2,1)} %reshape.95), calls=%async_computation.3 | async-start | bytes 524288 | tf_op jit(solution)/shard_map/all_to_all | solution.py:88
  277.4 5.9 %copy-start.1 = (bf16[512,4096]{0,1:T(8,128)(2,1)S(1)}, bf16[512,4096]{0,1:T(8,128)(2,1)}, u32[]{:S(2)}) copy-start(bf16[512,4096]{0,1:T(8,128)(2,1)} %copy.26) | copy-start | bytes 12582916
  285.1 21.1 %all-to-all-start.1 = ((bf16[32,2,2048]{2,1,0:T(2,128)(2,1)}), bf16[32,2,2048]{2,1,0:T(2,128)(2,1)S(1)}, u32[]{:S(2)}, u32[]{:S(2)}) async-start(bf16[32,2,2048]{2,1,0:T(2,128)(2,1)} %reshape.91), calls=%async_computation.1 | async-start | bytes 524288 | tf_op jit(solution)/shard_map/all_to_all | solution.py:88
Sparse Core Ops, SparseCore 0:
  9.9 85.5 all-gather.4
  98.2 85.9 all-gather.2
where the time goes:
time: 316 us; the launch traced here: 314 us
  waiting for transfers between devices  157 us (50%)
  matrix products  84.2 us (27%)
  starting transfers between devices  31.7 us (10%)
  local copies, waits for them, and re-layouts  23.1 us (7%)
  between operations  13.6 us (4%)
  other arithmetic  4.68 us (1%)
    all_gather x1, waiting for transfers between devices, local(): lax.all_gather(w_uq, 'dp', axis=0, tiled=True)  80.3 us
    dot_general x16, matrix products, one_head(): jnp.dot(operands[0], operands[1].T, preferred_element_type=jnp.float32)  44 us
    all_gather x1, waiting for transfers between devices, local(): lax.all_gather(w_ukv, 'dp', axis=0, tiled=True)  40.3 us
    all_to_all x2, waiting for transfers between devices, local(): lax.all_to_all(outgoing, 'dp', split_axis=0, concat_axis=0, tiled=True)  23.6 us
    dot_general x2, matrix products, local(): jnp.einsum('sq,hqc->shc', queries, absorbed, preferred_element_type=jnp.f...  21.5 us
    all_to_all x2, starting transfers between devices, local(): lax.all_to_all(outgoing, 'dp', split_axis=0, concat_axis=0, tiled=True)  16.3 us
    all_to_all x2, starting transfers between devices, local(): lax.all_to_all(head_out, 'dp', split_axis=0, concat_axis=0, tiled=True)  15.3 us
    all_to_all x2, waiting for transfers between devices, local(): lax.all_to_all(head_out, 'dp', split_axis=0, concat_axis=0, tiled=True)  11.1 us
  transfers between devices with their start and end apart: 6, of which 5 were waited for; matrix products, arithmetic and copies ran while one was open for 9% of the time, Pallas kernels for 0%

commit v1 on v0

v1 whole, which is shorter than its diff:
```python
import jax
import jax.numpy as jnp
from jax import lax
from jax.experimental import pallas as pl
from jax.experimental.pallas import tpu as pltpu
from jax.sharding import PartitionSpec as P

C = 512
NOPE = 128
QRANK = 1536
STEPS = 2
NY = 4
NZ = 8
NX = 4
HEADS = 16
SLOTS = 64
MAXLEN = 128
EXT = 144
ROWS = SLOTS * STEPS
COLS = HEADS * NOPE
HALF = COLS // 2
QUARTER = COLS // NY
PAYCOL = 256
MESH = pl.DeviceIdType.MESH
BF = jnp.bfloat16
F32 = jnp.float32


def iota(shape, dim):
    return lax.broadcasted_iota(jnp.int32, shape, dim)


def dot(a, b):
    return jnp.dot(a, b, preferred_element_type=F32)


def kernel(
    owners_ref, len_ref, uq_ref, ukv_ref, ql_ref, nl_ref, cache_ref, out_ref,
    pay, og, xf, wq, uk, kb, vb, ce, qs, qr, qa, mx, ob, rz, rs, ry,
    loc, xz_s, xz_r, xy_s, xy_r, xx_s, xx_r, xc_s, xc_r,
    wy_s, wy_r, wz_s, wz_r, kz_s, kz_r, ky_s, ky_r, vz_s, vz_r, vy_s, vy_r,
    q_s, q_r, oz_s, oz_r, oy_s, oy_r,
):
    dp = lax.axis_index("dp")
    hg = lax.axis_index("hg")
    y, z = dp // NZ, lax.rem(dp, NZ)
    x, c = hg // 2, lax.rem(hg, 2)

    def at_y(d):
        return lax.rem(y + (d + NY), NY)

    def at_z(d):
        return lax.rem(z + (d + NZ), NZ)

    def at_x(d):
        return lax.rem(x + (d + NX), NX)

    def dev_y(d):
        return (at_y(d) * NZ + z, hg)

    def dev_z(d):
        return (y * NZ + at_z(d), hg)

    def dev_x(d):
        return (dp, at_x(d) * 2 + c)

    sibling = (dp, x * 2 + (1 - c))
    sends = []

    def push(src, dst, send_sem, recv_sem, device):
        copy = pltpu.make_async_remote_copy(
            src_ref=src, dst_ref=dst, send_sem=send_sem, recv_sem=recv_sem,
            device_id=device, device_id_type=MESH,
        )
        copy.start()
        sends.append(copy)

    def arrived(dst, send_sem, recv_sem):
        pltpu.make_async_remote_copy(
            src_ref=dst, dst_ref=dst, send_sem=send_sem, recv_sem=recv_sem,
            device_id=sibling, device_id_type=MESH,
        ).wait_recv()

    barrier = pltpu.get_barrier_semaphore()
    peers = [dev_z(d) for d in range(1, NZ)] + [dev_y(d) for d in range(1, NY)]
    peers += [dev_x(d) for d in range(1, NX)] + [sibling]
    for peer in peers:
        pl.semaphore_signal(barrier, inc=1, device_id=peer, device_id_type=MESH)

    @pl.when(hg < 6)
    def _():
        pltpu.make_async_copy(
            ql_ref.at[:, :, pl.ds(pl.multiple_of(hg * PAYCOL, PAYCOL), PAYCOL)], pay, loc.at[0]
        ).start()

    @pl.when(hg >= 6)
    def _():
        pltpu.make_async_copy(
            nl_ref.at[:, :, pl.ds(pl.multiple_of((hg - 6) * PAYCOL, PAYCOL), PAYCOL)], pay, loc.at[0]
        ).start()

    ukv_in = pltpu.make_async_copy(ukv_ref, uk, loc.at[1])
    ukv_in.start()

    def uq_part(d):
        return uq_ref.at[:, pl.ds(pl.multiple_of(at_y(d) * QUARTER, QUARTER), QUARTER)]

    uq_in = pltpu.make_async_copy(uq_part(0), wq.at[y, z], loc.at[2])
    uq_in.start()
    cache_in = pltpu.make_async_copy(cache_ref, ce.at[:, pl.ds(0, MAXLEN), :], loc.at[3])
    cache_in.start()

    n = 2 * 32
    own_col = jnp.concatenate([owners_ref[...], owners_ref[...]], axis=0).astype(F32)
    row_i, col_i = iota((n, n), 0), iota((n, n), 1)
    eye = row_i == col_i
    own_row = jnp.sum(jnp.where(eye, own_col, 0.0), axis=0, keepdims=True)
    earlier = (own_col == own_row) & (col_i < row_i) & ((col_i // 32) == (row_i // 32))
    place = jnp.sum(jnp.where(earlier, 1.0, 0.0), axis=1, keepdims=True)
    dst_col = own_col * 2.0 + place
    dst_row = jnp.sum(jnp.where(eye, dst_col, 0.0), axis=0, keepdims=True)
    r0, c0 = iota((ROWS, n), 0), iota((ROWS, n), 1)
    want = ((lax.rem(r0 // 4, NY) * NZ + r0 // 16) * 2 + lax.rem(r0 // 2, 2)).astype(F32)
    spread = jnp.where((dst_row == want) & (c0 // 32 == lax.rem(r0, 2)), 1.0, 0.0).astype(BF)
    r1, c1 = iota((n, ROWS), 0), iota((n, ROWS), 1)
    collect = jnp.where(
        (dst_col == (c1 // 2).astype(F32)) & (r1 // 32 == lax.rem(c1, 2)), 1.0, 0.0
    ).astype(BF)
    r2, c2 = iota((ROWS, ROWS), 0), iota((ROWS, ROWS), 1)
    swap = jnp.where(
        c2 == lax.rem(r2 // 4, NZ) * 16 + (r2 // 32) * 4 + lax.rem(r2, 4), 1.0, 0.0
    ).astype(BF)
    r3, c3 = iota((256, ROWS), 0), iota((256, ROWS), 1)
    token = lax.rem(r3, 16)
    fresh_pick = jnp.where(
        (c3 == (r3 // 32) * 16 + y * 4 + lax.rem(r3 // 16, 2) * 2 + token) & (token < 2), 1.0, 0.0
    ).astype(BF)

    pltpu.make_async_copy(ql_ref.at[:, :, pl.ds(0, PAYCOL)], pay, loc.at[0]).wait()
    og[...] = dot(spread, pay[...].reshape(n, PAYCOL)).astype(BF)
    ukv_in.wait()
    for h in range(HEADS):
        cols = pl.ds(h * NOPE, NOPE)
        kb[y, z, :, cols] = uk[:, pl.ds(h * 256, 128)]
        vb[y, z, :, cols] = uk[:, pl.ds(h * 256 + 128, 128)]
    my_rows = pl.ds(pl.multiple_of(y * ROWS + z * 16, 16), 16)
    xf[hg, my_rows, :] = og[pl.ds(pl.multiple_of(z * 16, 16), 16), :]

    pl.semaphore_wait(barrier, len(peers))

    for d in range(1, NZ):
        push(
            og.at[pl.ds(pl.multiple_of(at_z(d) * 16, 16), 16), :], xf.at[hg, my_rows, :],
            xz_s.at[d], xz_r.at[d], dev_z(d),
        )
    for d in range(1, NY):
        push(uq_part(d), wq.at[y, z], wy_s.at[d], wy_r.at[d], dev_y(d))

    lo, hi = pl.ds(0, HALF), pl.ds(HALF, HALF)
    full = pl.ds(0, COLS)

    class Gather:
        def __init__(self, buf, z_s, z_r, y_s, y_r):
            self.buf, self.z_s, self.z_r, self.y_s, self.y_r = buf, z_s, z_r, y_s, y_r

        def block(self, dy, dz, cols=full):
            return self.buf.at[at_y(dy), at_z(dz), :, cols]

        def z_send(self, s):
            right = self.block(0, 1 - s, full if s < 4 else lo)
            push(right, right, self.z_s.at[s - 1], self.z_r.at[s - 1], dev_z(1))
            left = self.block(0, s - 1, full if s < 4 else hi)
            push(left, left, self.z_s.at[3 + s], self.z_r.at[3 + s], dev_z(-1))

        def z_wait(self, s):
            arrived(self.block(0, -s, full if s < 4 else lo), self.z_s.at[s - 1], self.z_r.at[s - 1])
            arrived(self.block(0, s, full if s < 4 else hi), self.z_s.at[3 + s], self.z_r.at[3 + s])

        def blocks(self, s):
            return [0] if s == 0 else [4] if s == 4 else [-s, s]

        def y_send(self, s):
            for dz in self.blocks(s):
                block, i = self.block(0, dz), (dz + NZ) % NZ
                push(block, block, self.y_s.at[i, 0], self.y_r.at[i, 0], dev_y(1))
                push(block, block, self.y_s.at[i, 1], self.y_r.at[i, 1], dev_y(-1))

        def y_relay(self, s):
            for dz in self.blocks(s):
                i = (dz + NZ) % NZ
                arrived(self.block(-1, dz), self.y_s.at[i, 0], self.y_r.at[i, 0])
                half = self.block(-1, dz, lo)
                push(half, half, self.y_s.at[i, 2], self.y_r.at[i, 2], dev_y(1))
                arrived(self.block(1, dz), self.y_s.at[i, 1], self.y_r.at[i, 1])
                half = self.block(1, dz, hi)
                push(half, half, self.y_s.at[i, 3], self.y_r.at[i, 3], dev_y(-1))

        def y_done(self, s):
            for dz in self.blocks(s):
                i = (dz + NZ) % NZ
                arrived(self.block(-2, dz, lo), self.y_s.at[i, 2], self.y_r.at[i, 2])
                arrived(self.block(2, dz, hi), self.y_s.at[i, 3], self.y_r.at[i, 3])

    keys = Gather(kb, kz_s, kz_r, ky_s, ky_r)
    values = Gather(vb, vz_s, vz_r, vy_s, vy_r)
    keys.z_send(1)
    keys.y_send(0)

    def xblock(dx, dy, core):
        return xf.at[
            at_x(dx) * 2 + core, pl.ds(pl.multiple_of(at_y(dy) * ROWS, ROWS), ROWS), :
        ]

    def share(dy):
        block = xblock(0, -dy, c)
        for d in range(1, NX):
            push(block, block, xx_s.at[dy, d], xx_r.at[dy, d], dev_x(d))
        push(block, block, xc_s.at[dy, 0], xc_r.at[dy, 0], sibling)

    for d in range(1, NZ):
        rows = pl.ds(pl.multiple_of(y * ROWS + at_z(-d) * 16, 16), 16)
        arrived(xf.at[hg, rows, :], xz_s.at[d], xz_r.at[d])
    for d in range(1, NY):
        push(xblock(0, 0, c), xblock(0, 0, c), xy_s.at[d], xy_r.at[d], dev_y(d))
    share(0)

    def wq_block(dz, part):
        return wq.at[part, at_z(dz)]

    all_y, low_y, high_y = pl.ds(0, NY), pl.ds(0, 2), pl.ds(2, 2)

    def wq_send(s):
        right = wq_block(1 - s, all_y if s < 4 else low_y)
        push(right, right, wz_s.at[s - 1], wz_r.at[s - 1], dev_z(1))
        left = wq_block(s - 1, all_y if s < 4 else high_y)
        push(left, left, wz_s.at[3 + s], wz_r.at[3 + s], dev_z(-1))

    def wq_wait(s):
        arrived(wq_block(-s, all_y if s < 4 else low_y), wz_s.at[s - 1], wz_r.at[s - 1])
        arrived(wq_block(s, all_y if s < 4 else high_y), wz_s.at[3 + s], wz_r.at[3 + s])

    uq_in.wait()
    for d in range(1, NY):
        arrived(wq.at[at_y(-d), z], wy_s.at[d], wy_r.at[d])
    wq_send(1)

    for s in range(1, 5):
        keys.z_wait(s)
        if s < 4:
            keys.z_send(s + 1)
        keys.y_send(s)
        if s == 1:
            for d in range(1, NY):
                arrived(xblock(0, -d, c), xy_s.at[d], xy_r.at[d])
                share(d)
        wq_wait(s)
        if s < 4:
            wq_send(s + 1)
        keys.y_relay(s - 1)
    values.z_send(1)
    values.y_send(0)
    for dy in range(NY):
        for d in range(1, NX):
            block = xblock(-d, -dy, c)
            arrived(block, xx_s.at[dy, d], xx_r.at[dy, d])
            push(block, block, xc_s.at[dy, d], xc_r.at[dy, d], sibling)
    keys.y_relay(4)
    for dy in range(NY):
        for d in range(NX):
            arrived(xblock(-d, -dy, 1 - c), xc_s.at[dy, d], xc_r.at[dy, d])

    total = None
    for p in range(2):
        lhs = jnp.concatenate([xf[3 * p + i] for i in range(3)], axis=1)
        part = dot(lhs, wq[pl.ds(2 * p, 2)].reshape(QRANK // 2, QUARTER))
        total = part if total is None else total + part
    query = total.astype(BF)
    for hy in range(NY):
        sorted_rows = dot(swap, query[hy * ROWS : (hy + 1) * ROWS]).astype(BF)
        for oy in range(NY):
            qs[oy, hy] = sorted_rows[oy * 32 : (oy + 1) * 32]
    for d in range(1, NY):
        push(qs.at[at_y(d)], qr.at[y], q_s.at[d], q_r.at[d], dev_y(d))
    qr[y] = qs[y]

    cache_in.wait()
    for hy in range(NY):
        rows = pl.ds(hy * ROWS, ROWS)
        fresh = jnp.concatenate([dot(fresh_pick, xf[6 + i, rows, :]) for i in range(2)], axis=1)
        ce[pl.ds(hy * 16, 16), pl.ds(MAXLEN, 16), :] = fresh.astype(BF).reshape(16, 16, C)

    for s in range(1, 4):
        values.z_wait(s)
        values.z_send(s + 1)
        values.y_send(s)
        values.y_relay(s - 1)
    for s in range(5):
        keys.y_done(s)
    for d in range(1, NY):
        arrived(qr.at[at_y(-d)], q_s.at[d], q_r.at[d])

    for h in range(HEADS):
        head_q = qr[h // 4, :, :, pl.ds((h % 4) * NOPE, NOPE)].reshape(ROWS, NOPE)
        head_k = kb[:, :, :, pl.ds(h * NOPE, NOPE)].reshape(C, NOPE)
        absorbed = lax.dot_general(
            head_q, head_k, (((1,), (1,)), ((), ())), preferred_element_type=F32
        )
        for l in range(4):
            qa[l, pl.ds(h, ROWS, stride=HEADS), :] = absorbed[:, l * 128 : (l + 1) * 128]

    values.z_wait(4)
    values.y_send(4)
    values.y_relay(3)

    column = iota((32, EXT), 1)
    second = iota((32, EXT), 0) >= HEADS
    new_ok = (column == MAXLEN) | ((column == MAXLEN + 1) & second)

    def attend(g, carry):
        scores, slots = [], []
        for hy in range(NY):
            for k in range(2):
                slot = (hy * NZ + g) * 2 + k
                slots.append(slot)
                rows = pl.ds(pl.multiple_of(slot * 32, 32), 32)
                a = jnp.concatenate([qa[l, rows, :] for l in range(4)], axis=1)
                s = lax.dot_general(
                    a.astype(BF), ce[slot], (((1,), (1,)), ((), ())),
                    preferred_element_type=F32,
                )
                ok = (column < len_ref[slot]) | new_ok
                scores.append(jnp.where(ok, s * (NOPE**-0.5), -1e30))
        s = jnp.concatenate(scores, axis=0)
        e = jnp.exp(s - jnp.max(s, axis=1, keepdims=True))
        w = (e / jnp.sum(e, axis=1, keepdims=True)).astype(BF)
        for i, slot in enumerate(slots):
            rows = pl.ds(pl.multiple_of((g * 8 + i) * 32, 32), 32)
            mixed = dot(w[i * 32 : (i + 1) * 32], ce[slot])
            for l in range(4):
                mx[l, rows, :] = mixed[:, l * 128 : (l + 1) * 128]
        return carry

    lax.fori_loop(0, NZ, attend, 0)

    values.y_relay(4)
    for s in range(5):
        values.y_done(s)

    parts = [lo, hi]
    for p, cols in enumerate(parts):
        for h in range(p * 8, p * 8 + 8):
            mixed = jnp.concatenate(
                [mx[l, pl.ds(h, ROWS, stride=HEADS), :] for l in range(4)], axis=1
            ).astype(BF)
            head_v = vb[:, :, :, pl.ds(h * NOPE, NOPE)].reshape(C, NOPE)
            ob[:, pl.ds(h * NOPE, NOPE)] = dot(mixed, head_v).astype(BF)
        for d in range(1, NZ):
            push(
                ob.at[pl.ds(pl.multiple_of(at_z(d) * 16, 16), 16), cols], rz.at[z, :, cols],
                oz_s.at[p, d], oz_r.at[p, d], dev_z(d),
            )
        rz[z, :, cols] = ob[pl.ds(pl.multiple_of(z * 16, 16), 16), cols]
    for p, cols in enumerate(parts):
        for d in range(1, NZ):
            arrived(rz.at[at_z(-d), :, cols], oz_s.at[p, d], oz_r.at[p, d])
        back = dot(swap, rz[:, :, cols].reshape(ROWS, HALF)).astype(BF)
        rs[:, :, cols] = back.reshape(NY, 32, HALF)
        for d in range(1, NY):
            push(rs.at[at_y(d), :, cols], ry.at[y, :, cols], oy_s.at[p, d], oy_r.at[p, d], dev_y(d))
        ry[y, :, cols] = rs[y, :, cols]
    for p, cols in enumerate(parts):
        for d in range(1, NY):
            arrived(ry.at[at_y(-d), :, cols], oy_s.at[p, d], oy_r.at[p, d])
        home = dot(collect, ry[:, :, cols].reshape(ROWS, HALF)).astype(BF)
        out_ref[:, :, cols] = home.reshape(STEPS, 32, HALF)

    for copy in sends:
        copy.wait_send()


def local(w_ukv, w_uq, query_latent, new_latent, latent_cache, cache_lengths, owners):
    dma = pltpu.SemaphoreType.DMA
    pairs = [(8,), (4,), (4, 4), (4, 4), (4,), (8,), (8,), (8, 4), (8,), (8, 4), (4,), (2, 8), (2, 4)]
    sems = [dma((4,))]
    for shape in pairs:
        sems += [dma(shape), dma(shape)]
    scratch = [
        pltpu.VMEM((2, 32, PAYCOL), BF),
        pltpu.VMEM((ROWS, PAYCOL), BF),
        pltpu.VMEM((8, NY * ROWS, PAYCOL), BF),
        pltpu.VMEM((NY, NZ, 48, QUARTER), BF),
        pltpu.VMEM((16, 2 * COLS), BF),
        pltpu.VMEM((NY, NZ, 16, COLS), BF),
        pltpu.VMEM((NY, NZ, 16, COLS), BF),
        pltpu.VMEM((SLOTS, EXT, C), BF),
        pltpu.VMEM((NY, NY, 32, QUARTER), BF),
        pltpu.VMEM((NY, NY, 32, QUARTER), BF),
        pltpu.VMEM((4, ROWS * HEADS, 128), F32),
        pltpu.VMEM((4, ROWS * HEADS, 128), F32),
        pltpu.VMEM((ROWS, COLS), BF),
        pltpu.VMEM((NZ, 16, COLS), BF),
        pltpu.VMEM((NY, 32, COLS), BF),
        pltpu.VMEM((NY, 32, COLS), BF),
    ]
    return pl.pallas_call(
        kernel,
        out_shape=jax.ShapeDtypeStruct((STEPS, 32, COLS), BF),
        in_specs=[
            pl.BlockSpec(memory_space=pltpu.VMEM),
            pl.BlockSpec(memory_space=pltpu.SMEM),
        ]
        + [pl.BlockSpec(memory_space=pl.ANY)] * 5,
        out_specs=pl.BlockSpec(memory_space=pltpu.VMEM),
        scratch_shapes=scratch + sems,
        compiler_params=pltpu.CompilerParams(
            collective_id=0, has_side_effects=True, vmem_limit_bytes=50 * 1024 * 1024
        ),
    )(owners, cache_lengths, w_uq, w_ukv, query_latent, new_latent, latent_cache)


def solution(mesh):
    in_specs = (
        P("dp", "hg"),
        P("dp", "hg"),
        P(None, "dp", None),
        P(None, "dp", None),
        P("dp", None, None),
        P("dp"),
        P("dp", None),
    )
    out_specs = P(None, "dp", "hg")
    return jax.shard_map(local, mesh=mesh, in_specs=in_specs, out_specs=out_specs, check_vma=False)
```

time: 316 us -> 98.5 us (0.31)
  waiting for transfers between devices: 157 us -> 0 us
  Pallas kernels: 0 us -> 92.6 us
  matrix products: 84.2 us -> 0 us
  starting transfers between devices: 31.7 us -> 0 us
  local copies, waits for them, and re-layouts: 23.1 us -> 5.69 us
  between operations: 13.6 us -> 0.01 us
  other arithmetic: 4.68 us -> 0 us
    all_gather x2 -> x0, waiting for transfers between devices: 121 us -> none  [the longest x1 80.3 us: local(): lax.all_gather(w_uq, 'dp', axis=0, tiled=True)]
    pallas_call x0 -> x1, Pallas kernels: none -> 92.6 us  [local(): pl.pallas_call(kernel, out_shape=jax.ShapeDtypeStruct((STEPS, 32, COLS),...]
    dot_general x31 -> x0, matrix products: 84.2 us -> none  [the longest x16 44 us: one_head(): jnp.dot(operands[0], operands[1].T, preferred_element_type=jnp.float32)]
    all_to_all x4 -> x0, waiting for transfers between devices: 34.7 us -> none  [the longest x2 23.6 us: local(): lax.all_to_all(outgoing, 'dp', split_axis=0, concat_axis=0, tiled=True)]
    all_to_all x4 -> x0, starting transfers between devices: 31.6 us -> none  [the longest x2 16.3 us: local(): lax.all_to_all(outgoing, 'dp', split_axis=0, concat_axis=0, tiled=True)]
    all_gather x2 -> x0, local copies, waits for them, and re-layouts: 15.1 us -> none  [the longest x1 8.6 us: local(): lax.all_gather(w_uq, 'dp', axis=0, tiled=True)]
    unnamed x8 -> x12, local copies, waits for them, and re-layouts: 0.41 us -> 5.69 us
    reshape x8 -> x0, local copies, waits for them, and re-layouts: 3.71 us -> none  [the longest x2 1.79 us: local(): outgoing = outgoing.reshape(dp_count, send_cap, QRANK + C)]
  transfers between devices with their start and end apart: 6 -> 0, of which waited for: 5 -> 0; matrix products, arithmetic and copies ran while one was open for 9% -> 0% of each run, Pallas kernels for 0% -> 0%
where the time goes in v1:
time: 98.5 us; the launch traced here: 98.3 us
  Pallas kernels  92.6 us (94%)
  local copies, waits for them, and re-layouts  5.69 us (6%)
    pallas_call x1, Pallas kernels, local(): pl.pallas_call(kernel, out_shape=jax.ShapeDtypeStruct((STEPS, 32, COLS),...  92.6 us
    unnamed x12, local copies, waits for them, and re-layouts  5.69 us

profile of v1, /device:TPU:2, one launch (start us, length us, event | category | flops | bytes accessed | tf_op | source)
XLA Modules:
  0.0 98.3 jit_solution(17628523505724293906)
XLA Ops:
  0.0 0.7 copy.8.owners_ref
  0.7 0.0 copy-start
  0.7 0.9 copy-done
  1.7 0.0 copy-start.1
  1.7 0.9 copy-done.1
  2.6 0.0 copy-start.2
  2.6 0.9 copy-done.2
  3.5 0.0 copy-start.3
  3.5 0.8 copy-done.3
  4.3 0.0 copy-start.4
  4.3 0.7 copy-done.4
  5.0 92.6 %shard_map.73 = bf16[2,32,2048]{2,1,0:T(8,128)(2,1)S(1)} custom-call(s32[32,1]{1,0:T(8,128)S(1)} %copy.8.owners_ref, s32[64]{0:T(128)S(1)} %copy-done.4, bf16[48,2048]{1,0:T(8,128)(2,1)S(1)} %copy-done, bf16[16,4096]{1,0:T(8,128)(2,1)S(1)} %copy-done.2, bf16[2,32,1536]{2,1,0:T(8,128)(2,1)S(1)} %copy-done.1, bf16[2,32,512]{2,1,0:T(8,128)(2,1)S(1)} %copy-done.3, ...), custom_call_target="tpu_custom_call" | custom-call | tf_op jit(solution)/shard_map/pallas_call | solution.py:405
  97.6 0.7 copy.10
Async XLA Ops:
  0.7 0.9 copy-start
  1.7 0.9 copy-start.1
  2.6 0.9 copy-start.2
  3.5 0.8 copy-start.3
  4.3 0.7 copy-start.4
